TPU v7x, 32 devices: a whole 2x2x4 slice. The times are simulated.
32 devices in a mesh: ty: 8 (over z, x), tx: 4 (over y, core).
Axes of the slice: x: 2, y: 2, z: 4, core: 2. Of those that a mesh axis runs over, the one named last changes fastest.
Arguments:
- fixed_image: float32 [512, 1024], P('ty', 'tx'), may hold values from -6 to 6
- moving_image: float32 [512, 1024], P('ty', 'tx'), may hold values from -6 to 6
- tissue: int32 [16, 32], P('ty', 'tx'), may hold values from 0 to 1, as said below
Outputs:
- coefficients: float32 [2, 16, 32], P(None, 'ty', 'tx')
- mismatch: float32 [512, 1024], P('ty', 'tx')
Inputs may be any that keep to these rules, and one draw needn't show every extreme that they name: 1 marks a block of 32 x 32 fine pixels that holds tissue, 0 background.
All inputs are finite; a program needn't handle non-finite values.
Results may differ from a plain program's by a relative error of at most 0.0003.
Values sent between devices are 32-bit elements; how exact they have to be, the bound alone decides.
A program may use at most 64 MiB of HBM per device.

v0:
```python
import jax
import jax.numpy as jnp
from jax import lax
from jax.sharding import PartitionSpec as P

SPACE = 32
HALO = 6
MB = 32
ITERS = 2
offset_pairs = (
    (0, 2),
    (0, -2),
    (2, 0),
    (-2, 0),
    (2, 2),
    (2, -2),
    (-2, 2),
    (-2, -2),
    (0, 4),
    (0, -4),
    (4, 0),
    (-4, 0),
)
highest = lax.Precision.HIGHEST


def with_halo(block, sides, width):
    for axis, dim in sides:
        count = lax.axis_size(axis)
        forward = [(i, i + 1) for i in range(count - 1)]
        backward = [(target, source) for source, target in forward]
        low = lax.ppermute(
            lax.slice_in_dim(block, block.shape[dim] - width, None, axis=dim), axis, forward
        )
        high = lax.ppermute(lax.slice_in_dim(block, 0, width, axis=dim), axis, backward)
        block = jnp.concatenate([low, block, high], axis=dim)
    return block


def bspline(values):
    magnitude = jnp.abs(values)
    near_part = 2.0 / 3.0 - magnitude * magnitude + 0.5 * magnitude**3
    far_part = (2.0 - magnitude) ** 3 / 6.0
    return jnp.where(
        magnitude < 1.0, near_part, jnp.where(magnitude < 2.0, far_part, 0.0 * magnitude)
    )


def box_mean(values):
    height, breadth = values.shape
    total = values[0 : height - 2, 0 : breadth - 2]
    for shift_y in range(3):
        for shift_x in range(3):
            if shift_y + shift_x > 0:
                total = (
                    total + values[shift_y : height - 2 + shift_y, shift_x : breadth - 2 + shift_x]
                )
    return total / 9.0


def descriptors(padded):
    height, breadth = padded.shape
    centre = padded[4 : height - 4, 4 : breadth - 4]
    distances = []
    for offset_y, offset_x in offset_pairs:
        shifted = padded[
            4 + offset_y : height - 4 + offset_y, 4 + offset_x : breadth - 4 + offset_x
        ]
        distances.append(box_mean((centre - shifted) ** 2))
    variance = sum(distances) / 12.0 + 0.1
    return [jnp.exp(-member / variance) for member in distances]


def level_terms(fixed_padded, moving_padded, factor):
    fixed_mind = descriptors(fixed_padded)
    moving_mind = descriptors(moving_padded)
    summed = None
    for fixed_part, moving_part in zip(fixed_mind, moving_mind):
        differ = moving_part[1:-1, 1:-1] - fixed_part[1:-1, 1:-1]
        slope_y = (moving_part[2:, 1:-1] - moving_part[:-2, 1:-1]) / (2.0 * factor)
        slope_x = (moving_part[1:-1, 2:] - moving_part[1:-1, :-2]) / (2.0 * factor)
        parts = (
            differ * slope_y,
            differ * slope_x,
            slope_y * slope_y,
            slope_y * slope_x,
            slope_x * slope_x,
            differ * differ,
        )
        summed = (
            parts if summed is None else tuple((left + right for left, right in zip(summed, parts)))
        )
    return summed


def window_matrix(length, factor, cell_count):
    position = factor * jnp.arange(length, dtype=jnp.float32) + (factor - 1) / 2.0
    knots = jnp.arange(cell_count + 3, dtype=jnp.float32) - 1.0
    return bspline(position[:, None] / SPACE - knots[None, :])


def expand_mask(tissue, factor):
    side = MB // factor
    block_rows, block_cols = tissue.shape
    spread = jnp.broadcast_to(
        tissue.astype(jnp.float32)[:, None, :, None], (block_rows, side, block_cols, side)
    )
    return spread.reshape(block_rows * side, block_cols * side)


def pool_stack(images):
    planes, height, breadth = images.shape
    return images.reshape(planes, height // 2, 2, breadth // 2, 2).mean(axis=(2, 4))


def sandwich(left, values, right):
    return jnp.einsum("pa,cab,qb->cpq", left, values, right, precision=highest)


def gradient_terms(summed, weight, field):
    return jnp.stack(
        [
            weight * (summed[0] + summed[2] * field[0] + summed[3] * field[1]),
            weight * (summed[1] + summed[3] * field[0] + summed[4] * field[1]),
        ]
    )


def curvature_density(summed, weight, motion):
    return weight * (
        motion[0] * (summed[2] * motion[0] + summed[3] * motion[1])
        + motion[1] * (summed[3] * motion[0] + summed[4] * motion[1])
    )


def mismatch_of(summed, field):
    return (
        summed[5]
        + 2.0 * (summed[0] * field[0] + summed[1] * field[1])
        + field[0] * (summed[2] * field[0] + summed[3] * field[1])
        + field[1] * (summed[3] * field[0] + summed[4] * field[1])
    )


def window_of(control):
    padded = with_halo(control, (("ty", 1), ("tx", 2)), 2)
    return padded[:, 1:, 1:]


def fold_rim(padded, along, length):
    own_part = lax.slice_in_dim(padded, 4, 4 + length, axis=along)
    from_above = lax.slice_in_dim(padded, 1, 3, axis=along)
    from_below = lax.slice_in_dim(padded, length + 6, length + 7, axis=along)
    above_widths = [(0, 0), (0, 0), (0, 0)]
    above_widths[along] = (0, length - 2)
    below_widths = [(0, 0), (0, 0), (0, 0)]
    below_widths[along] = (length - 1, 0)
    return own_part + jnp.pad(from_above, above_widths) + jnp.pad(from_below, below_widths)


def run_level(padded, weight, coefficients, factor, start_zero):
    summed = level_terms(padded[0], padded[1], factor)
    height, breadth = summed[0].shape
    cells_y = height * factor // SPACE
    cells_x = breadth * factor // SPACE
    rows_window = window_matrix(height, factor, cells_y)
    cols_window = window_matrix(breadth, factor, cells_x)
    if start_zero:
        field = jnp.zeros((2, height, breadth), jnp.float32)
    else:
        field = sandwich(rows_window, window_of(coefficients), cols_window)
    for iteration in range(ITERS):
        pixel_grad = gradient_terms(summed, weight, field)
        partial_grad = sandwich(rows_window.T, pixel_grad, cols_window.T)
        spilled = with_halo(partial_grad, (("ty", 1), ("tx", 2)), 3)
        direction = fold_rim(fold_rim(spilled, 1, cells_y), 2, cells_x)
        motion = sandwich(rows_window, window_of(direction), cols_window)
        norm_sum, curvature = lax.psum(
            (jnp.sum(direction * direction), jnp.sum(curvature_density(summed, weight, motion))),
            ("ty", "tx"),
        )
        step_size = norm_sum / curvature
        coefficients = coefficients - step_size * direction
        field = field - step_size * motion
    return (coefficients, field, summed)


def shards(fixed_image, moving_image, tissue):
    stacked = jnp.stack([fixed_image, moving_image])
    fine_padded = with_halo(stacked, (("ty", 1), ("tx", 2)), HALO)
    coarse_padded = with_halo(pool_stack(stacked), (("ty", 1), ("tx", 2)), HALO)
    cells_y = fixed_image.shape[0] // SPACE
    cells_x = fixed_image.shape[1] // SPACE
    coefficients = jnp.zeros((2, cells_y, cells_x), jnp.float32)
    coefficients, field, summed = run_level(
        coarse_padded, expand_mask(tissue, 2), coefficients, 2, True
    )
    coefficients, field, summed = run_level(
        fine_padded, expand_mask(tissue, 1), coefficients, 1, False
    )
    return (coefficients, mismatch_of(summed, field))


def solution(mesh):
    placed = (P("ty", "tx"), P("ty", "tx"), P("ty", "tx"))
    return jax.shard_map(
        shards,
        mesh=mesh,
        in_specs=placed,
        out_specs=(P(None, "ty", "tx"), P("ty", "tx")),
        check_vma=False,
    )
```

profile of v0, /device:TPU:0, one launch (start us, length us, event | category | flops | bytes accessed | tf_op | source)
XLA Modules:
  0.0 384.1 jit_solution(11618381650321247970)
XLA Ops:
  0.6 6.3 %stack.52 = f32[1,32,2,128,2]{4,3,2,1,0:T(8,128)} reshape(f32[64,256]{1,0:T(8,128)} %param.4) | data formatting | bytes 131072 | tf_op jit(solution)/shard_map/stack | solution.py:189
  7.0 2.8 copy.6
  9.8 5.6 %stack.51 = f32[1,32,2,128,2]{4,3,2,1,0:T(8,128)} reshape(f32[64,256]{1,0:T(8,128)S(1)} %copy-done.1) | data formatting | bytes 131072 | tf_op jit(solution)/shard_map/stack | solution.py:189
  15.4 2.8 copy.5
  18.3 1.3 collective-permute-start.1
  19.6 5.5 %collective-permute-start = (f32[2,6,128]{2,1,0:T(8,128)S(1)}, f32[2,6,128]{2,1,0:T(8,128)S(1)}, u32[]{:S(2)}, u32[]{:S(2)}) collective-permute-start(f32[2,6,128]{2,1,0:T(8,128)S(1)} %get-tuple-element.180), channel_id=1, source_target_pairs={{0,4},{4,8},{8,12},{12,16},{16,20},{20,24},{24,28},{1,5},{5,9},{9,... | collective-permute-start | bytes 18440 | tf_op jit(solution)/shard_map/ppermute | solution.py:32
  25.1 1.3 collective-permute-done
  26.5 1.3 collective-permute-start.3
  27.8 3.0 collective-permute-start.2
  35.3 1.3 collective-permute-start.5
  36.6 5.4 %collective-permute-start.4 = (f32[2,3,11]{2,1,0:T(4,128)S(1)}, f32[2,3,11]{2,1,0:T(4,128)S(1)}, u32[]{:S(2)}, u32[]{:S(2)}) collective-permute-start(f32[2,3,11]{2,1,0:T(4,128)S(1)} %get-tuple-element.206), channel_id=1, source_target_pairs={{0,4},{4,8},{8,12},{12,16},{16,20},{20,24},{24,28},{1,5},{5,9},{9,... | collective-permute-start | bytes 800 | tf_op jit(solution)/shard_map/ppermute | solution.py:32
  42.0 1.3 collective-permute-done.4
  43.4 1.3 collective-permute-start.7
  44.7 3.1 collective-permute-start.6
  50.9 5.7 %collective-permute-start.8 = (f32[2,2,8]{2,1,0:T(2,128)S(1)}, f32[2,2,8]{2,1,0:T(2,128)S(1)}, u32[]{:S(2)}, u32[]{:S(2)}) collective-permute-start(f32[2,2,8]{2,1,0:T(2,128)S(1)} %get-tuple-element.36), channel_id=1, source_target_pairs={{0,4},{4,8},{8,12},{12,16},{16,20},{20,24},{24,28},{1,5},{5,9},{9,... | collective-permute-start | bytes 392 | tf_op jit(solution)/shard_map/ppermute | solution.py:32
  58.0 1.3 collective-permute-start.11
  59.2 4.9 %collective-permute-start.10 = (f32[2,6,2]{2,1,0:T(8,128)S(1)}, f32[2,6,2]{2,1,0:T(8,128)S(1)}, u32[]{:S(2)}, u32[]{:S(2)}) collective-permute-start(f32[2,6,2]{2,1,0:T(8,128)S(1)} %get-tuple-element.204), channel_id=1, source_target_pairs={{0,1},{1,2},{2,3},{4,5},{5,6},{6,7},{8,9},{9,10},{10,11},{12,13},{... | collective-permute-start | bytes 296 | tf_op jit(solution)/shard_map/ppermute | solution.py:32
  66.1 47.5 %all-reduce.15 = (f32[]{:T(128)}, f32[]{:T(128)}) all-reduce(f32[]{:T(128)} %get-tuple-element.35, f32[]{:T(128)} %multiply_reduce_fusion.3), channel_id=1, replica_groups=mesh['ty'=8,'tx'=4] {'ty','tx'}, use_global_device_ids=true, to_apply=%region_2.3 | all-reduce | flops 2 | bytes 16 | tf_op jit(solution)/shard_map/psum | solution.py:178
  115.4 1.3 collective-permute-start.13
  116.7 4.8 %collective-permute-start.12 = (f32[2,3,11]{2,1,0:T(4,128)S(1)}, f32[2,3,11]{2,1,0:T(4,128)S(1)}, u32[]{:S(2)}, u32[]{:S(2)}) collective-permute-start(f32[2,3,11]{2,1,0:T(4,128)S(1)} %get-tuple-element.202), channel_id=1, source_target_pairs={{0,4},{4,8},{8,12},{12,16},{16,20},{20,24},{24,28},{1,5},{5,9},{9,... | collective-permute-start | bytes 800 | tf_op jit(solution)/shard_map/ppermute | solution.py:32
  121.6 1.3 collective-permute-start.21
  122.9 5.5 %collective-permute-start.20 = (f32[2,6,256]{2,1,0:T(8,128)S(1)}, f32[2,6,256]{2,1,0:T(8,128)S(1)}, u32[]{:S(2)}, u32[]{:S(2)}) collective-permute-start(f32[2,6,256]{2,1,0:T(8,128)S(1)} %get-tuple-element.102), channel_id=1, source_target_pairs={{0,4},{4,8},{8,12},{12,16},{16,20},{20,24},{24,28},{1,5},{5,9},{9,... | collective-permute-start | bytes 36872 | tf_op jit(solution)/shard_map/ppermute | solution.py:32
  128.4 1.3 collective-permute-start.15
  129.7 3.0 collective-permute-start.14
  135.8 5.4 %collective-permute-start.16 = (f32[2,2,8]{2,1,0:T(2,128)S(1)}, f32[2,2,8]{2,1,0:T(2,128)S(1)}, u32[]{:S(2)}, u32[]{:S(2)}) collective-permute-start(f32[2,2,8]{2,1,0:T(2,128)S(1)} %get-tuple-element.34), channel_id=1, source_target_pairs={{0,4},{4,8},{8,12},{12,16},{16,20},{20,24},{24,28},{1,5},{5,9},{9,... | collective-permute-start | bytes 392 | tf_op jit(solution)/shard_map/ppermute | solution.py:32
  143.9 3.4 collective-permute-start.18
  149.3 46.0 %all-reduce.14 = (f32[]{:T(128)}, f32[]{:T(128)}) all-reduce(f32[]{:T(128)} %get-tuple-element.33, f32[]{:T(128)} %multiply_reduce_fusion.2), channel_id=1, replica_groups=mesh['ty'=8,'tx'=4] {'ty','tx'}, use_global_device_ids=true, to_apply=%region_6.7 | all-reduce | flops 2 | bytes 16 | tf_op jit(solution)/shard_map/psum | solution.py:178
  196.7 1.3 collective-permute-start.25
  198.0 4.8 %collective-permute-start.24 = (f32[2,2,8]{2,1,0:T(2,128)S(1)}, f32[2,2,8]{2,1,0:T(2,128)S(1)}, u32[]{:S(2)}, u32[]{:S(2)}) collective-permute-start(f32[2,2,8]{2,1,0:T(2,128)S(1)} %multiply_subtract_fusion.4), channel_id=1, source_target_pairs={{0,4},{4,8},{8,12},{12,16},{16,20},{20,24},{24,28},{1,5},{5,9},{9,... | collective-permute-start | bytes 392 | tf_op jit(solution)/shard_map/ppermute | solution.py:32
  205.5 3.0 collective-permute-start.26
  209.7 1.3 collective-permute-start.23
  211.0 4.5 %collective-permute-start.22 = (f32[2,76,6]{2,1,0:T(8,128)S(1)}, f32[2,76,6]{2,1,0:T(8,128)S(1)}, u32[]{:S(2)}, u32[]{:S(2)}) collective-permute-start(f32[2,76,6]{2,1,0:T(8,128)S(1)} %get-tuple-element.100), channel_id=1, source_target_pairs={{0,1},{1,2},{2,3},{4,5},{5,6},{6,7},{8,9},{9,10},{10,11},{12,13},{... | collective-permute-start | bytes 10952 | tf_op jit(solution)/shard_map/ppermute | solution.py:32
  217.4 2.1 divide_exponential_fusion
  219.7 2.1 multiply_add_fusion
  224.0 1.3 collective-permute-start.29
  225.3 5.4 %collective-permute-start.28 = (f32[2,3,11]{2,1,0:T(4,128)S(1)}, f32[2,3,11]{2,1,0:T(4,128)S(1)}, u32[]{:S(2)}, u32[]{:S(2)}) collective-permute-start(f32[2,3,11]{2,1,0:T(4,128)S(1)} %get-tuple-element.196), channel_id=1, source_target_pairs={{0,4},{4,8},{8,12},{12,16},{16,20},{20,24},{24,28},{1,5},{5,9},{9,... | collective-permute-start | bytes 800 | tf_op jit(solution)/shard_map/ppermute | solution.py:32
  230.7 1.3 collective-permute-done.28
  233.4 4.5 %collective-permute-start.30 = (f32[2,11,3]{2,1,0:T(8,128)S(1)}, f32[2,11,3]{2,1,0:T(8,128)S(1)}, u32[]{:S(2)}, u32[]{:S(2)}) collective-permute-start(f32[2,11,3]{2,1,0:T(8,128)S(1)} %get-tuple-element.184), channel_id=1, source_target_pairs={{0,1},{1,2},{2,3},{4,5},{5,6},{6,7},{8,9},{9,10},{10,11},{12,13},{... | collective-permute-start | bytes 800 | tf_op jit(solution)/shard_map/ppermute | solution.py:32
  241.0 5.7 %collective-permute-start.32 = (f32[2,2,8]{2,1,0:T(2,128)S(1)}, f32[2,2,8]{2,1,0:T(2,128)S(1)}, u32[]{:S(2)}, u32[]{:S(2)}) collective-permute-start(f32[2,2,8]{2,1,0:T(2,128)S(1)} %get-tuple-element.13), channel_id=1, source_target_pairs={{0,4},{4,8},{8,12},{12,16},{16,20},{20,24},{24,28},{1,5},{5,9},{9,... | collective-permute-start | bytes 392 | tf_op jit(solution)/shard_map/ppermute | solution.py:32
  249.3 4.9 %collective-permute-start.34 = (f32[2,6,2]{2,1,0:T(8,128)S(1)}, f32[2,6,2]{2,1,0:T(8,128)S(1)}, u32[]{:S(2)}, u32[]{:S(2)}) collective-permute-start(f32[2,6,2]{2,1,0:T(8,128)S(1)} %get-tuple-element.194), channel_id=1, source_target_pairs={{0,1},{1,2},{2,3},{4,5},{5,6},{6,7},{8,9},{9,10},{10,11},{12,13},{... | collective-permute-start | bytes 296 | tf_op jit(solution)/shard_map/ppermute | solution.py:32
  256.4 47.4 %all-reduce.13 = (f32[]{:T(128)}, f32[]{:T(128)}) all-reduce(f32[]{:T(128)} %get-tuple-element.12, f32[]{:T(128)} %multiply_reduce_fusion.1), channel_id=1, replica_groups=mesh['ty'=8,'tx'=4] {'ty','tx'}, use_global_device_ids=true, to_apply=%region_10.11 | all-reduce | flops 2 | bytes 16 | tf_op jit(solution)/shard_map/psum | solution.py:178
  305.6 1.3 collective-permute-start.37
  306.9 4.8 %collective-permute-start.36 = (f32[2,3,11]{2,1,0:T(4,128)S(1)}, f32[2,3,11]{2,1,0:T(4,128)S(1)}, u32[]{:S(2)}, u32[]{:S(2)}) collective-permute-start(f32[2,3,11]{2,1,0:T(4,128)S(1)} %get-tuple-element.192), channel_id=1, source_target_pairs={{0,4},{4,8},{8,12},{12,16},{16,20},{20,24},{24,28},{1,5},{5,9},{9,... | collective-permute-start | bytes 800 | tf_op jit(solution)/shard_map/ppermute | solution.py:32
  311.7 1.3 collective-permute-done.36
  314.4 3.0 collective-permute-start.38
  320.5 5.4 %collective-permute-start.40 = (f32[2,2,8]{2,1,0:T(2,128)S(1)}, f32[2,2,8]{2,1,0:T(2,128)S(1)}, u32[]{:S(2)}, u32[]{:S(2)}) collective-permute-start(f32[2,2,8]{2,1,0:T(2,128)S(1)} %get-tuple-element.11), channel_id=1, source_target_pairs={{0,4},{4,8},{8,12},{12,16},{16,20},{20,24},{24,28},{1,5},{5,9},{9,... | collective-permute-start | bytes 392 | tf_op jit(solution)/shard_map/ppermute | solution.py:32
  328.6 3.5 collective-permute-start.42
  334.2 47.2 %all-reduce.12 = (f32[]{:T(128)}, f32[]{:T(128)}) all-reduce(f32[]{:T(128)} %get-tuple-element.10, f32[]{:T(128)} %multiply_reduce_fusion), channel_id=1, replica_groups=mesh['ty'=8,'tx'=4] {'ty','tx'}, use_global_device_ids=true, to_apply=%region_14.15 | all-reduce | flops 2 | bytes 16 | tf_op jit(solution)/shard_map/psum | solution.py:178
  (161 shorter events, 46.9 us)
Async XLA Ops:
  0.6 9.2 %copy-start.1 = (f32[64,256]{1,0:T(8,128)S(1)}, f32[64,256]{1,0:T(8,128)}, u32[]{:S(2)}) copy-start(f32[64,256]{1,0:T(8,128)} %param.3) | copy-start | bytes 196612
  9.8 21.0 %copy-start.2 = (s32[2,8]{1,0:T(2,128)S(1)}, s32[2,8]{1,0:T(2,128)}, u32[]{:S(2)}) copy-start(s32[2,8]{1,0:T(2,128)} %param.5) | copy-start | bytes 196
  18.3 6.8 %collective-permute-start.1 = (f32[2,6,128]{2,1,0:T(8,128)S(1)}, f32[2,6,128]{2,1,0:T(8,128)S(1)}, u32[]{:S(2)}, u32[]{:S(2)}) collective-permute-start(f32[2,6,128]{2,1,0:T(8,128)S(1)} %get-tuple-element.181), channel_id=1, source_target_pairs={{4,0},{8,4},{12,8},{16,12},{20,16},{24,20},{28,24},{5,1},{9,5},{13... | collective-permute-start | bytes 18440 | tf_op jit(solution)/shard_map/ppermute | solution.py:35
  19.6 6.8 %collective-permute-start = (f32[2,6,128]{2,1,0:T(8,128)S(1)}, f32[2,6,128]{2,1,0:T(8,128)S(1)}, u32[]{:S(2)}, u32[]{:S(2)}) collective-permute-start(f32[2,6,128]{2,1,0:T(8,128)S(1)} %get-tuple-element.180), channel_id=1, source_target_pairs={{0,4},{4,8},{8,12},{12,16},{16,20},{20,24},{24,28},{1,5},{5,9},{9,... | collective-permute-start | bytes 18440 | tf_op jit(solution)/shard_map/ppermute | solution.py:32
  26.5 4.6 %collective-permute-start.3 = (f32[2,44,6]{2,1,0:T(8,128)S(1)}, f32[2,44,6]{2,1,0:T(8,128)S(1)}, u32[]{:S(2)}, u32[]{:S(2)}) collective-permute-start(f32[2,44,6]{2,1,0:T(8,128)S(1)} %get-tuple-element.168), channel_id=1, source_target_pairs={{1,0},{2,1},{3,2},{5,4},{6,5},{7,6},{9,8},{10,9},{11,10},{13,12},{... | collective-permute-start | bytes 6344 | tf_op jit(solution)/shard_map/ppermute | solution.py:35
  27.8 3.9 %collective-permute-start.2 = (f32[2,44,6]{2,1,0:T(8,128)S(1)}, f32[2,44,6]{2,1,0:T(8,128)S(1)}, u32[]{:S(2)}, u32[]{:S(2)}) collective-permute-start(f32[2,44,6]{2,1,0:T(8,128)S(1)} %get-tuple-element.167), channel_id=1, source_target_pairs={{0,1},{1,2},{2,3},{4,5},{5,6},{6,7},{8,9},{9,10},{10,11},{12,13},{... | collective-permute-start | bytes 6344 | tf_op jit(solution)/shard_map/ppermute | solution.py:32
  33.2 23.4 %copy-start = (f32[64,256]{1,0:T(8,128)S(1)}, f32[64,256]{1,0:T(8,128)}, u32[]{:S(2)}) copy-start(f32[64,256]{1,0:T(8,128)} %param.4) | copy-start | bytes 196612
  35.3 6.8 %collective-permute-start.5 = (f32[2,3,11]{2,1,0:T(4,128)S(1)}, f32[2,3,11]{2,1,0:T(4,128)S(1)}, u32[]{:S(2)}, u32[]{:S(2)}) collective-permute-start(f32[2,3,11]{2,1,0:T(4,128)S(1)} %get-tuple-element.207), channel_id=1, source_target_pairs={{4,0},{8,4},{12,8},{16,12},{20,16},{24,20},{28,24},{5,1},{9,5},{13... | collective-permute-start | bytes 800 | tf_op jit(solution)/shard_map/ppermute | solution.py:35
  36.6 6.8 %collective-permute-start.4 = (f32[2,3,11]{2,1,0:T(4,128)S(1)}, f32[2,3,11]{2,1,0:T(4,128)S(1)}, u32[]{:S(2)}, u32[]{:S(2)}) collective-permute-start(f32[2,3,11]{2,1,0:T(4,128)S(1)} %get-tuple-element.206), channel_id=1, source_target_pairs={{0,4},{4,8},{8,12},{12,16},{16,20},{20,24},{24,28},{1,5},{5,9},{9,... | collective-permute-start | bytes 800 | tf_op jit(solution)/shard_map/ppermute | solution.py:32
  43.4 4.4 %collective-permute-start.7 = (f32[2,11,3]{2,1,0:T(8,128)S(1)}, f32[2,11,3]{2,1,0:T(8,128)S(1)}, u32[]{:S(2)}, u32[]{:S(2)}) collective-permute-start(f32[2,11,3]{2,1,0:T(8,128)S(1)} %get-tuple-element.189), channel_id=1, source_target_pairs={{1,0},{2,1},{3,2},{5,4},{6,5},{7,6},{9,8},{10,9},{11,10},{13,12},{... | collective-permute-start | bytes 800 | tf_op jit(solution)/shard_map/ppermute | solution.py:35
  44.7 3.9 %collective-permute-start.6 = (f32[2,11,3]{2,1,0:T(8,128)S(1)}, f32[2,11,3]{2,1,0:T(8,128)S(1)}, u32[]{:S(2)}, u32[]{:S(2)}) collective-permute-start(f32[2,11,3]{2,1,0:T(8,128)S(1)} %get-tuple-element.188), channel_id=1, source_target_pairs={{0,1},{1,2},{2,3},{4,5},{5,6},{6,7},{8,9},{9,10},{10,11},{12,13},{... | collective-permute-start | bytes 800 | tf_op jit(solution)/shard_map/ppermute | solution.py:32
  49.6 7.0 %collective-permute-start.9 = (f32[2,2,8]{2,1,0:T(2,128)S(1)}, f32[2,2,8]{2,1,0:T(2,128)S(1)}, u32[]{:S(2)}, u32[]{:S(2)}) collective-permute-start(f32[2,2,8]{2,1,0:T(2,128)S(1)} %get-tuple-element.36), channel_id=1, source_target_pairs={{4,0},{8,4},{12,8},{16,12},{20,16},{24,20},{28,24},{5,1},{9,5},{13... | collective-permute-start | bytes 392 | tf_op jit(solution)/shard_map/ppermute | solution.py:35
  50.9 7.0 %collective-permute-start.8 = (f32[2,2,8]{2,1,0:T(2,128)S(1)}, f32[2,2,8]{2,1,0:T(2,128)S(1)}, u32[]{:S(2)}, u32[]{:S(2)}) collective-permute-start(f32[2,2,8]{2,1,0:T(2,128)S(1)} %get-tuple-element.36), channel_id=1, source_target_pairs={{0,4},{4,8},{8,12},{12,16},{16,20},{20,24},{24,28},{1,5},{5,9},{9,... | collective-permute-start | bytes 392 | tf_op jit(solution)/shard_map/ppermute | solution.py:32
  58.0 6.2 %collective-permute-start.11 = (f32[2,6,2]{2,1,0:T(8,128)S(1)}, f32[2,6,2]{2,1,0:T(8,128)S(1)}, u32[]{:S(2)}, u32[]{:S(2)}) collective-permute-start(f32[2,6,2]{2,1,0:T(8,128)S(1)} %get-tuple-element.205), channel_id=1, source_target_pairs={{1,0},{2,1},{3,2},{5,4},{6,5},{7,6},{9,8},{10,9},{11,10},{13,12},{... | collective-permute-start | bytes 296 | tf_op jit(solution)/shard_map/ppermute | solution.py:35
  59.2 5.7 %collective-permute-start.10 = (f32[2,6,2]{2,1,0:T(8,128)S(1)}, f32[2,6,2]{2,1,0:T(8,128)S(1)}, u32[]{:S(2)}, u32[]{:S(2)}) collective-permute-start(f32[2,6,2]{2,1,0:T(8,128)S(1)} %get-tuple-element.204), channel_id=1, source_target_pairs={{0,1},{1,2},{2,3},{4,5},{5,6},{6,7},{8,9},{9,10},{10,11},{12,13},{... | collective-permute-start | bytes 296 | tf_op jit(solution)/shard_map/ppermute | solution.py:32
  115.4 12.9 %collective-permute-start.13 = (f32[2,3,11]{2,1,0:T(4,128)S(1)}, f32[2,3,11]{2,1,0:T(4,128)S(1)}, u32[]{:S(2)}, u32[]{:S(2)}) collective-permute-start(f32[2,3,11]{2,1,0:T(4,128)S(1)} %get-tuple-element.203), channel_id=1, source_target_pairs={{4,0},{8,4},{12,8},{16,12},{20,16},{24,20},{28,24},{5,1},{9,5},{13... | collective-permute-start | bytes 800 | tf_op jit(solution)/shard_map/ppermute | solution.py:35
  116.7 11.6 %collective-permute-start.12 = (f32[2,3,11]{2,1,0:T(4,128)S(1)}, f32[2,3,11]{2,1,0:T(4,128)S(1)}, u32[]{:S(2)}, u32[]{:S(2)}) collective-permute-start(f32[2,3,11]{2,1,0:T(4,128)S(1)} %get-tuple-element.202), channel_id=1, source_target_pairs={{0,4},{4,8},{8,12},{12,16},{16,20},{20,24},{24,28},{1,5},{5,9},{9,... | collective-permute-start | bytes 800 | tf_op jit(solution)/shard_map/ppermute | solution.py:32
  121.6 88.0 %collective-permute-start.21 = (f32[2,6,256]{2,1,0:T(8,128)S(1)}, f32[2,6,256]{2,1,0:T(8,128)S(1)}, u32[]{:S(2)}, u32[]{:S(2)}) collective-permute-start(f32[2,6,256]{2,1,0:T(8,128)S(1)} %get-tuple-element.103), channel_id=1, source_target_pairs={{4,0},{8,4},{12,8},{16,12},{20,16},{24,20},{28,24},{5,1},{9,5},{13... | collective-permute-start | bytes 36872 | tf_op jit(solution)/shard_map/ppermute | solution.py:35
  122.9 86.7 %collective-permute-start.20 = (f32[2,6,256]{2,1,0:T(8,128)S(1)}, f32[2,6,256]{2,1,0:T(8,128)S(1)}, u32[]{:S(2)}, u32[]{:S(2)}) collective-permute-start(f32[2,6,256]{2,1,0:T(8,128)S(1)} %get-tuple-element.102), channel_id=1, source_target_pairs={{0,4},{4,8},{8,12},{12,16},{16,20},{20,24},{24,28},{1,5},{5,9},{9,... | collective-permute-start | bytes 36872 | tf_op jit(solution)/shard_map/ppermute | solution.py:32
  128.4 4.3 %collective-permute-start.15 = (f32[2,11,3]{2,1,0:T(8,128)S(1)}, f32[2,11,3]{2,1,0:T(8,128)S(1)}, u32[]{:S(2)}, u32[]{:S(2)}) collective-permute-start(f32[2,11,3]{2,1,0:T(8,128)S(1)} %get-tuple-element.187), channel_id=1, source_target_pairs={{1,0},{2,1},{3,2},{5,4},{6,5},{7,6},{9,8},{10,9},{11,10},{13,12},{... | collective-permute-start | bytes 800 | tf_op jit(solution)/shard_map/ppermute | solution.py:35
  129.7 3.9 %collective-permute-start.14 = (f32[2,11,3]{2,1,0:T(8,128)S(1)}, f32[2,11,3]{2,1,0:T(8,128)S(1)}, u32[]{:S(2)}, u32[]{:S(2)}) collective-permute-start(f32[2,11,3]{2,1,0:T(8,128)S(1)} %get-tuple-element.186), channel_id=1, source_target_pairs={{0,1},{1,2},{2,3},{4,5},{5,6},{6,7},{8,9},{9,10},{10,11},{12,13},{... | collective-permute-start | bytes 800 | tf_op jit(solution)/shard_map/ppermute | solution.py:32
  134.5 6.8 %collective-permute-start.17 = (f32[2,2,8]{2,1,0:T(2,128)S(1)}, f32[2,2,8]{2,1,0:T(2,128)S(1)}, u32[]{:S(2)}, u32[]{:S(2)}) collective-permute-start(f32[2,2,8]{2,1,0:T(2,128)S(1)} %get-tuple-element.34), channel_id=1, source_target_pairs={{4,0},{8,4},{12,8},{16,12},{20,16},{24,20},{28,24},{5,1},{9,5},{13... | collective-permute-start | bytes 392 | tf_op jit(solution)/shard_map/ppermute | solution.py:35
  135.8 6.7 %collective-permute-start.16 = (f32[2,2,8]{2,1,0:T(2,128)S(1)}, f32[2,2,8]{2,1,0:T(2,128)S(1)}, u32[]{:S(2)}, u32[]{:S(2)}) collective-permute-start(f32[2,2,8]{2,1,0:T(2,128)S(1)} %get-tuple-element.34), channel_id=1, source_target_pairs={{0,4},{4,8},{8,12},{12,16},{16,20},{20,24},{24,28},{1,5},{5,9},{9,... | collective-permute-start | bytes 392 | tf_op jit(solution)/shard_map/ppermute | solution.py:32
  142.6 4.7 %collective-permute-start.19 = (f32[2,6,2]{2,1,0:T(8,128)S(1)}, f32[2,6,2]{2,1,0:T(8,128)S(1)}, u32[]{:S(2)}, u32[]{:S(2)}) collective-permute-start(f32[2,6,2]{2,1,0:T(8,128)S(1)} %get-tuple-element.201), channel_id=1, source_target_pairs={{1,0},{2,1},{3,2},{5,4},{6,5},{7,6},{9,8},{10,9},{11,10},{13,12},{... | collective-permute-start | bytes 296 | tf_op jit(solution)/shard_map/ppermute | solution.py:35
  143.9 4.2 %collective-permute-start.18 = (f32[2,6,2]{2,1,0:T(8,128)S(1)}, f32[2,6,2]{2,1,0:T(8,128)S(1)}, u32[]{:S(2)}, u32[]{:S(2)}) collective-permute-start(f32[2,6,2]{2,1,0:T(8,128)S(1)} %get-tuple-element.200), channel_id=1, source_target_pairs={{0,1},{1,2},{2,3},{4,5},{5,6},{6,7},{8,9},{9,10},{10,11},{12,13},{... | collective-permute-start | bytes 296 | tf_op jit(solution)/shard_map/ppermute | solution.py:32
  196.7 6.3 %collective-permute-start.25 = (f32[2,2,8]{2,1,0:T(2,128)S(1)}, f32[2,2,8]{2,1,0:T(2,128)S(1)}, u32[]{:S(2)}, u32[]{:S(2)}) collective-permute-start(f32[2,2,8]{2,1,0:T(2,128)S(1)} %multiply_subtract_fusion.4), channel_id=1, source_target_pairs={{4,0},{8,4},{12,8},{16,12},{20,16},{24,20},{28,24},{5,1},{9,5},{13... | collective-permute-start | bytes 392 | tf_op jit(solution)/shard_map/ppermute | solution.py:35
  198.0 6.1 %collective-permute-start.24 = (f32[2,2,8]{2,1,0:T(2,128)S(1)}, f32[2,2,8]{2,1,0:T(2,128)S(1)}, u32[]{:S(2)}, u32[]{:S(2)}) collective-permute-start(f32[2,2,8]{2,1,0:T(2,128)S(1)} %multiply_subtract_fusion.4), channel_id=1, source_target_pairs={{0,4},{4,8},{8,12},{12,16},{16,20},{20,24},{24,28},{1,5},{5,9},{9,... | collective-permute-start | bytes 392 | tf_op jit(solution)/shard_map/ppermute | solution.py:32
  204.2 4.3 %collective-permute-start.27 = (f32[2,6,2]{2,1,0:T(8,128)S(1)}, f32[2,6,2]{2,1,0:T(8,128)S(1)}, u32[]{:S(2)}, u32[]{:S(2)}) collective-permute-start(f32[2,6,2]{2,1,0:T(8,128)S(1)} %get-tuple-element.199), channel_id=1, source_target_pairs={{1,0},{2,1},{3,2},{5,4},{6,5},{7,6},{9,8},{10,9},{11,10},{13,12},{... | collective-permute-start | bytes 296 | tf_op jit(solution)/shard_map/ppermute | solution.py:35
  205.5 3.8 %collective-permute-start.26 = (f32[2,6,2]{2,1,0:T(8,128)S(1)}, f32[2,6,2]{2,1,0:T(8,128)S(1)}, u32[]{:S(2)}, u32[]{:S(2)}) collective-permute-start(f32[2,6,2]{2,1,0:T(8,128)S(1)} %get-tuple-element.198), channel_id=1, source_target_pairs={{0,1},{1,2},{2,3},{4,5},{5,6},{6,7},{8,9},{9,10},{10,11},{12,13},{... | collective-permute-start | bytes 296 | tf_op jit(solution)/shard_map/ppermute | solution.py:32
  209.7 6.2 %collective-permute-start.23 = (f32[2,76,6]{2,1,0:T(8,128)S(1)}, f32[2,76,6]{2,1,0:T(8,128)S(1)}, u32[]{:S(2)}, u32[]{:S(2)}) collective-permute-start(f32[2,76,6]{2,1,0:T(8,128)S(1)} %get-tuple-element.101), channel_id=1, source_target_pairs={{1,0},{2,1},{3,2},{5,4},{6,5},{7,6},{9,8},{10,9},{11,10},{13,12},{... | collective-permute-start | bytes 10952 | tf_op jit(solution)/shard_map/ppermute | solution.py:35
  211.0 5.2 %collective-permute-start.22 = (f32[2,76,6]{2,1,0:T(8,128)S(1)}, f32[2,76,6]{2,1,0:T(8,128)S(1)}, u32[]{:S(2)}, u32[]{:S(2)}) collective-permute-start(f32[2,76,6]{2,1,0:T(8,128)S(1)} %get-tuple-element.100), channel_id=1, source_target_pairs={{0,1},{1,2},{2,3},{4,5},{5,6},{6,7},{8,9},{9,10},{10,11},{12,13},{... | collective-permute-start | bytes 10952 | tf_op jit(solution)/shard_map/ppermute | solution.py:32
  224.0 6.7 %collective-permute-start.29 = (f32[2,3,11]{2,1,0:T(4,128)S(1)}, f32[2,3,11]{2,1,0:T(4,128)S(1)}, u32[]{:S(2)}, u32[]{:S(2)}) collective-permute-start(f32[2,3,11]{2,1,0:T(4,128)S(1)} %get-tuple-element.197), channel_id=1, source_target_pairs={{4,0},{8,4},{12,8},{16,12},{20,16},{24,20},{28,24},{5,1},{9,5},{13... | collective-permute-start | bytes 800 | tf_op jit(solution)/shard_map/ppermute | solution.py:35
  225.3 6.7 %collective-permute-start.28 = (f32[2,3,11]{2,1,0:T(4,128)S(1)}, f32[2,3,11]{2,1,0:T(4,128)S(1)}, u32[]{:S(2)}, u32[]{:S(2)}) collective-permute-start(f32[2,3,11]{2,1,0:T(4,128)S(1)} %get-tuple-element.196), channel_id=1, source_target_pairs={{0,4},{4,8},{8,12},{12,16},{16,20},{20,24},{24,28},{1,5},{5,9},{9,... | collective-permute-start | bytes 800 | tf_op jit(solution)/shard_map/ppermute | solution.py:32
  232.1 5.8 %collective-permute-start.31 = (f32[2,11,3]{2,1,0:T(8,128)S(1)}, f32[2,11,3]{2,1,0:T(8,128)S(1)}, u32[]{:S(2)}, u32[]{:S(2)}) collective-permute-start(f32[2,11,3]{2,1,0:T(8,128)S(1)} %get-tuple-element.185), channel_id=1, source_target_pairs={{1,0},{2,1},{3,2},{5,4},{6,5},{7,6},{9,8},{10,9},{11,10},{13,12},{... | collective-permute-start | bytes 800 | tf_op jit(solution)/shard_map/ppermute | solution.py:35
  233.4 5.4 %collective-permute-start.30 = (f32[2,11,3]{2,1,0:T(8,128)S(1)}, f32[2,11,3]{2,1,0:T(8,128)S(1)}, u32[]{:S(2)}, u32[]{:S(2)}) collective-permute-start(f32[2,11,3]{2,1,0:T(8,128)S(1)} %get-tuple-element.184), channel_id=1, source_target_pairs={{0,1},{1,2},{2,3},{4,5},{5,6},{6,7},{8,9},{9,10},{10,11},{12,13},{... | collective-permute-start | bytes 800 | tf_op jit(solution)/shard_map/ppermute | solution.py:32
  239.7 7.0 %collective-permute-start.33 = (f32[2,2,8]{2,1,0:T(2,128)S(1)}, f32[2,2,8]{2,1,0:T(2,128)S(1)}, u32[]{:S(2)}, u32[]{:S(2)}) collective-permute-start(f32[2,2,8]{2,1,0:T(2,128)S(1)} %get-tuple-element.13), channel_id=1, source_target_pairs={{4,0},{8,4},{12,8},{16,12},{20,16},{24,20},{28,24},{5,1},{9,5},{13... | collective-permute-start | bytes 392 | tf_op jit(solution)/shard_map/ppermute | solution.py:35
  241.0 7.0 %collective-permute-start.32 = (f32[2,2,8]{2,1,0:T(2,128)S(1)}, f32[2,2,8]{2,1,0:T(2,128)S(1)}, u32[]{:S(2)}, u32[]{:S(2)}) collective-permute-start(f32[2,2,8]{2,1,0:T(2,128)S(1)} %get-tuple-element.13), channel_id=1, source_target_pairs={{0,4},{4,8},{8,12},{12,16},{16,20},{20,24},{24,28},{1,5},{5,9},{9,... | collective-permute-start | bytes 392 | tf_op jit(solution)/shard_map/ppermute | solution.py:32
  248.1 6.2 %collective-permute-start.35 = (f32[2,6,2]{2,1,0:T(8,128)S(1)}, f32[2,6,2]{2,1,0:T(8,128)S(1)}, u32[]{:S(2)}, u32[]{:S(2)}) collective-permute-start(f32[2,6,2]{2,1,0:T(8,128)S(1)} %get-tuple-element.195), channel_id=1, source_target_pairs={{1,0},{2,1},{3,2},{5,4},{6,5},{7,6},{9,8},{10,9},{11,10},{13,12},{... | collective-permute-start | bytes 296 | tf_op jit(solution)/shard_map/ppermute | solution.py:35
  249.3 5.8 %collective-permute-start.34 = (f32[2,6,2]{2,1,0:T(8,128)S(1)}, f32[2,6,2]{2,1,0:T(8,128)S(1)}, u32[]{:S(2)}, u32[]{:S(2)}) collective-permute-start(f32[2,6,2]{2,1,0:T(8,128)S(1)} %get-tuple-element.194), channel_id=1, source_target_pairs={{0,1},{1,2},{2,3},{4,5},{5,6},{6,7},{8,9},{9,10},{10,11},{12,13},{... | collective-permute-start | bytes 296 | tf_op jit(solution)/shard_map/ppermute | solution.py:32
  305.6 6.1 %collective-permute-start.37 = (f32[2,3,11]{2,1,0:T(4,128)S(1)}, f32[2,3,11]{2,1,0:T(4,128)S(1)}, u32[]{:S(2)}, u32[]{:S(2)}) collective-permute-start(f32[2,3,11]{2,1,0:T(4,128)S(1)} %get-tuple-element.193), channel_id=1, source_target_pairs={{4,0},{8,4},{12,8},{16,12},{20,16},{24,20},{28,24},{5,1},{9,5},{13... | collective-permute-start | bytes 800 | tf_op jit(solution)/shard_map/ppermute | solution.py:35
  306.9 6.1 %collective-permute-start.36 = (f32[2,3,11]{2,1,0:T(4,128)S(1)}, f32[2,3,11]{2,1,0:T(4,128)S(1)}, u32[]{:S(2)}, u32[]{:S(2)}) collective-permute-start(f32[2,3,11]{2,1,0:T(4,128)S(1)} %get-tuple-element.192), channel_id=1, source_target_pairs={{0,4},{4,8},{8,12},{12,16},{16,20},{20,24},{24,28},{1,5},{5,9},{9,... | collective-permute-start | bytes 800 | tf_op jit(solution)/shard_map/ppermute | solution.py:32
  313.1 4.3 %collective-permute-start.39 = (f32[2,11,3]{2,1,0:T(8,128)S(1)}, f32[2,11,3]{2,1,0:T(8,128)S(1)}, u32[]{:S(2)}, u32[]{:S(2)}) collective-permute-start(f32[2,11,3]{2,1,0:T(8,128)S(1)} %get-tuple-element.183), channel_id=1, source_target_pairs={{1,0},{2,1},{3,2},{5,4},{6,5},{7,6},{9,8},{10,9},{11,10},{13,12},{... | collective-permute-start | bytes 800 | tf_op jit(solution)/shard_map/ppermute | solution.py:35
  314.4 3.9 %collective-permute-start.38 = (f32[2,11,3]{2,1,0:T(8,128)S(1)}, f32[2,11,3]{2,1,0:T(8,128)S(1)}, u32[]{:S(2)}, u32[]{:S(2)}) collective-permute-start(f32[2,11,3]{2,1,0:T(8,128)S(1)} %get-tuple-element.182), channel_id=1, source_target_pairs={{0,1},{1,2},{2,3},{4,5},{5,6},{6,7},{8,9},{9,10},{10,11},{12,13},{... | collective-permute-start | bytes 800 | tf_op jit(solution)/shard_map/ppermute | solution.py:32
  319.2 6.7 %collective-permute-start.41 = (f32[2,2,8]{2,1,0:T(2,128)S(1)}, f32[2,2,8]{2,1,0:T(2,128)S(1)}, u32[]{:S(2)}, u32[]{:S(2)}) collective-permute-start(f32[2,2,8]{2,1,0:T(2,128)S(1)} %get-tuple-element.11), channel_id=1, source_target_pairs={{4,0},{8,4},{12,8},{16,12},{20,16},{24,20},{28,24},{5,1},{9,5},{13... | collective-permute-start | bytes 392 | tf_op jit(solution)/shard_map/ppermute | solution.py:35
  320.5 6.7 %collective-permute-start.40 = (f32[2,2,8]{2,1,0:T(2,128)S(1)}, f32[2,2,8]{2,1,0:T(2,128)S(1)}, u32[]{:S(2)}, u32[]{:S(2)}) collective-permute-start(f32[2,2,8]{2,1,0:T(2,128)S(1)} %get-tuple-element.11), channel_id=1, source_target_pairs={{0,4},{4,8},{8,12},{12,16},{16,20},{20,24},{24,28},{1,5},{5,9},{9,... | collective-permute-start | bytes 392 | tf_op jit(solution)/shard_map/ppermute | solution.py:32
  327.3 4.8 %collective-permute-start.43 = (f32[2,6,2]{2,1,0:T(8,128)S(1)}, f32[2,6,2]{2,1,0:T(8,128)S(1)}, u32[]{:S(2)}, u32[]{:S(2)}) collective-permute-start(f32[2,6,2]{2,1,0:T(8,128)S(1)} %get-tuple-element.191), channel_id=1, source_target_pairs={{1,0},{2,1},{3,2},{5,4},{6,5},{7,6},{9,8},{10,9},{11,10},{13,12},{... | collective-permute-start | bytes 296 | tf_op jit(solution)/shard_map/ppermute | solution.py:35
  328.6 4.3 %collective-permute-start.42 = (f32[2,6,2]{2,1,0:T(8,128)S(1)}, f32[2,6,2]{2,1,0:T(8,128)S(1)}, u32[]{:S(2)}, u32[]{:S(2)}) collective-permute-start(f32[2,6,2]{2,1,0:T(8,128)S(1)} %get-tuple-element.190), channel_id=1, source_target_pairs={{0,1},{1,2},{2,3},{4,5},{5,6},{6,7},{8,9},{9,10},{10,11},{12,13},{... | collective-permute-start | bytes 296 | tf_op jit(solution)/shard_map/ppermute | solution.py:32
where the time goes:
time: 386 us; the launch traced here: 384 us
  blocking collectives  188 us (49%)
  starting transfers between devices  128 us (33%)
  waiting for transfers between devices  19.6 us (5%)
  local copies, waits for them, and re-layouts  19.5 us (5%)
  other arithmetic  17.5 us (5%)
  between operations  6.96 us (2%)
  matrix products  4.67 us (1%)
    psum x4, blocking collectives, run_level(): lax.psum((jnp.sum(direction * direction), jnp.sum(curvature_density(summe...  188 us
    ppermute x22, starting transfers between devices, with_halo(): lax.ppermute(lax.slice_in_dim(block, block.shape[dim] - width, None, axis...  99.5 us
    ppermute x22, starting transfers between devices, with_halo(): lax.ppermute(lax.slice_in_dim(block, 0, width, axis=dim), axis, backward)  28.3 us
    ppermute x22, waiting for transfers between devices, with_halo(): lax.ppermute(lax.slice_in_dim(block, block.shape[dim] - width, None, axis...  19.5 us
    another operation x4, local copies, waits for them, and re-layouts, shards(): stacked = jnp.stack([fixed_image, moving_image])  17.6 us
  transfers between devices with their start and end apart: 44, of which 20 were waited for; matrix products, arithmetic and copies ran while one was open for 1% of the time, Pallas kernels for 0%

commit v1 on v0

--- a/solution.py
+++ b/solution.py
@@ -176,8 +176,14 @@
         direction = fold_rim(fold_rim(spilled, 1, cells_y), 2, cells_x)
         motion = sandwich(rows_window, window_of(direction), cols_window)
         norm_sum, curvature = lax.psum(
-            (jnp.sum(direction * direction), jnp.sum(curvature_density(summed, weight, motion))),
-            ("ty", "tx"),
+            lax.psum(
+                (
+                    jnp.sum(direction * direction),
+                    jnp.sum(curvature_density(summed, weight, motion)),
+                ),
+                "tx",
+            ),
+            "ty",
         )
         step_size = norm_sum / curvature
         coefficients = coefficients - step_size * direction

time: 386 us -> 320 us (0.83)
  blocking collectives: 188 us -> 128 us
  starting transfers between devices: 128 us -> 123 us
    psum x4, blocking collectives: 188 us -> 39.2 us  [run_level(): lax.psum((jnp.sum(direction * direction), jnp.sum(curvature_density(summe...]
    psum x0 -> x4, blocking collectives: none -> 88.5 us  [run_level(): lax.psum(lax.psum((jnp.sum(direction * direction), jnp.sum(curvature_dens...]
    ppermute x22, starting transfers between devices: 99.5 us -> 94.5 us  [with_halo(): lax.ppermute(lax.slice_in_dim(block, block.shape[dim] - width, None, axis...]
where the time goes in v1:
time: 320 us; the launch traced here: 319 us
  blocking collectives  128 us (40%)
  starting transfers between devices  123 us (38%)
  waiting for transfers between devices  19.6 us (6%)
  local copies, waits for them, and re-layouts  19.4 us (6%)
  other arithmetic  17.5 us (5%)
  between operations  6.96 us (2%)
  matrix products  4.67 us (1%)
    ppermute x22, starting transfers between devices, with_halo(): lax.ppermute(lax.slice_in_dim(block, block.shape[dim] - width, None, axis...  94.5 us
    psum x4, blocking collectives, run_level(): lax.psum(lax.psum((jnp.sum(direction * direction), jnp.sum(curvature_dens...  88.5 us
    psum x4, blocking collectives, run_level(): lax.psum((jnp.sum(direction * direction), jnp.sum(curvature_density(summe...  39.2 us
    ppermute x22, starting transfers between devices, with_halo(): lax.ppermute(lax.slice_in_dim(block, 0, width, axis=dim), axis, backward)  28.3 us
    ppermute x22, waiting for transfers between devices, with_halo(): lax.ppermute(lax.slice_in_dim(block, block.shape[dim] - width, None, axis...  19.5 us
    another operation x4, local copies, waits for them, and re-layouts, shards(): stacked = jnp.stack([fixed_image, moving_image])  17.5 us
  transfers between devices with their start and end apart: 44, of which 20 were waited for; matrix products, arithmetic and copies ran while one was open for 1% of the time, Pallas kernels for 0%

profile of v1, /device:TPU:0, one launch (start us, length us, event | category | flops | bytes accessed | tf_op | source)
XLA Modules:
  0.0 318.6 jit_solution(17011929733056365030)
XLA Ops:
  0.6 6.3 %stack.52 = f32[1,32,2,128,2]{4,3,2,1,0:T(8,128)} reshape(f32[64,256]{1,0:T(8,128)} %param.4) | data formatting | bytes 131072 | tf_op jit(solution)/shard_map/stack | solution.py:195
  7.0 2.8 copy.6
  9.8 5.5 %stack.51 = f32[1,32,2,128,2]{4,3,2,1,0:T(8,128)} reshape(f32[64,256]{1,0:T(8,128)S(1)} %copy-done.1) | data formatting | bytes 131072 | tf_op jit(solution)/shard_map/stack | solution.py:195
  15.4 2.8 copy.5
  18.3 1.3 collective-permute-start.1
  19.6 5.5 %collective-permute-start = (f32[2,6,128]{2,1,0:T(8,128)S(1)}, f32[2,6,128]{2,1,0:T(8,128)S(1)}, u32[]{:S(2)}, u32[]{:S(2)}) collective-permute-start(f32[2,6,128]{2,1,0:T(8,128)S(1)} %get-tuple-element.188), channel_id=1, source_target_pairs={{0,4},{4,8},{8,12},{12,16},{16,20},{20,24},{24,28},{1,5},{5,9},{9,... | collective-permute-start | bytes 18440 | tf_op jit(solution)/shard_map/ppermute | solution.py:32
  25.1 1.3 collective-permute-done
  27.8 3.0 collective-permute-start.2
  35.2 1.3 collective-permute-start.5
  36.5 5.4 %collective-permute-start.4 = (f32[2,3,11]{2,1,0:T(4,128)S(1)}, f32[2,3,11]{2,1,0:T(4,128)S(1)}, u32[]{:S(2)}, u32[]{:S(2)}) collective-permute-start(f32[2,3,11]{2,1,0:T(4,128)S(1)} %get-tuple-element.214), channel_id=1, source_target_pairs={{0,4},{4,8},{8,12},{12,16},{16,20},{20,24},{24,28},{1,5},{5,9},{9,... | collective-permute-start | bytes 800 | tf_op jit(solution)/shard_map/ppermute | solution.py:32
  42.0 1.3 collective-permute-done.4
  44.7 3.1 collective-permute-start.6
  50.8 5.7 %collective-permute-start.8 = (f32[2,2,8]{2,1,0:T(2,128)S(1)}, f32[2,2,8]{2,1,0:T(2,128)S(1)}, u32[]{:S(2)}, u32[]{:S(2)}) collective-permute-start(f32[2,2,8]{2,1,0:T(2,128)S(1)} %get-tuple-element.44), channel_id=1, source_target_pairs={{0,4},{4,8},{8,12},{12,16},{16,20},{20,24},{24,28},{1,5},{5,9},{9,... | collective-permute-start | bytes 392 | tf_op jit(solution)/shard_map/ppermute | solution.py:32
  59.2 4.9 %collective-permute-start.10 = (f32[2,6,2]{2,1,0:T(8,128)S(1)}, f32[2,6,2]{2,1,0:T(8,128)S(1)}, u32[]{:S(2)}, u32[]{:S(2)}) collective-permute-start(f32[2,6,2]{2,1,0:T(8,128)S(1)} %get-tuple-element.212), channel_id=1, source_target_pairs={{0,1},{1,2},{2,3},{4,5},{5,6},{6,7},{8,9},{9,10},{10,11},{12,13},{... | collective-permute-start | bytes 296 | tf_op jit(solution)/shard_map/ppermute | solution.py:32
  66.1 9.7 %all-reduce.19 = (f32[]{:T(128)}, f32[]{:T(128)}) all-reduce(f32[]{:T(128)} %get-tuple-element.43, f32[]{:T(128)} %multiply_reduce_fusion.3), channel_id=1, replica_groups=mesh['ty'=8,'tx'=4] {'tx'}, use_global_device_ids=true, to_apply=%region_2.3 | all-reduce | flops 2 | bytes 16 | tf_op jit(solution)/shard_map/psum | solution.py:179
  75.8 25.2 %all-reduce.15 = (f32[]{:T(128)}, f32[]{:T(128)}) all-reduce(f32[]{:T(128)} %get-tuple-element.16, f32[]{:T(128)} %get-tuple-element.17), channel_id=1, replica_groups=mesh['ty'=8,'tx'=4] {'ty'}, use_global_device_ids=true, to_apply=%region_3.4 | all-reduce | flops 2 | bytes 16 | tf_op jit(solution)/shard_map/psum | solution.py:178
  102.8 1.3 collective-permute-start.13
  104.1 4.5 %collective-permute-start.12 = (f32[2,3,11]{2,1,0:T(4,128)S(1)}, f32[2,3,11]{2,1,0:T(4,128)S(1)}, u32[]{:S(2)}, u32[]{:S(2)}) collective-permute-start(f32[2,3,11]{2,1,0:T(4,128)S(1)} %get-tuple-element.210), channel_id=1, source_target_pairs={{0,4},{4,8},{8,12},{12,16},{16,20},{20,24},{24,28},{1,5},{5,9},{9,... | collective-permute-start | bytes 800 | tf_op jit(solution)/shard_map/ppermute | solution.py:32
  108.7 1.3 collective-permute-start.21
  110.0 4.5 %collective-permute-start.20 = (f32[2,6,256]{2,1,0:T(8,128)S(1)}, f32[2,6,256]{2,1,0:T(8,128)S(1)}, u32[]{:S(2)}, u32[]{:S(2)}) collective-permute-start(f32[2,6,256]{2,1,0:T(8,128)S(1)} %get-tuple-element.110), channel_id=1, source_target_pairs={{0,4},{4,8},{8,12},{12,16},{16,20},{20,24},{24,28},{1,5},{5,9},{9,... | collective-permute-start | bytes 36872 | tf_op jit(solution)/shard_map/ppermute | solution.py:32
  115.9 3.0 collective-permute-start.14
  122.0 4.5 %collective-permute-start.16 = (f32[2,2,8]{2,1,0:T(2,128)S(1)}, f32[2,2,8]{2,1,0:T(2,128)S(1)}, u32[]{:S(2)}, u32[]{:S(2)}) collective-permute-start(f32[2,2,8]{2,1,0:T(2,128)S(1)} %get-tuple-element.42), channel_id=1, source_target_pairs={{0,4},{4,8},{8,12},{12,16},{16,20},{20,24},{24,28},{1,5},{5,9},{9,... | collective-permute-start | bytes 392 | tf_op jit(solution)/shard_map/ppermute | solution.py:32
  129.2 3.0 collective-permute-start.18
  134.2 9.9 %all-reduce.18 = (f32[]{:T(128)}, f32[]{:T(128)}) all-reduce(f32[]{:T(128)} %get-tuple-element.41, f32[]{:T(128)} %multiply_reduce_fusion.2), channel_id=1, replica_groups=mesh['ty'=8,'tx'=4] {'tx'}, use_global_device_ids=true, to_apply=%region_8.9 | all-reduce | flops 2 | bytes 16 | tf_op jit(solution)/shard_map/psum | solution.py:179
  144.2 20.0 %all-reduce.14 = (f32[]{:T(128)}, f32[]{:T(128)}) all-reduce(f32[]{:T(128)} %get-tuple-element.14, f32[]{:T(128)} %get-tuple-element.15), channel_id=1, replica_groups=mesh['ty'=8,'tx'=4] {'ty'}, use_global_device_ids=true, to_apply=%region_9.10 | all-reduce | flops 2 | bytes 16 | tf_op jit(solution)/shard_map/psum | solution.py:178
  165.6 1.3 collective-permute-start.25
  166.9 4.5 %collective-permute-start.24 = (f32[2,2,8]{2,1,0:T(2,128)S(1)}, f32[2,2,8]{2,1,0:T(2,128)S(1)}, u32[]{:S(2)}, u32[]{:S(2)}) collective-permute-start(f32[2,2,8]{2,1,0:T(2,128)S(1)} %multiply_subtract_fusion.4), channel_id=1, source_target_pairs={{0,4},{4,8},{8,12},{12,16},{16,20},{20,24},{24,28},{1,5},{5,9},{9,... | collective-permute-start | bytes 392 | tf_op jit(solution)/shard_map/ppermute | solution.py:32
  174.1 3.0 collective-permute-start.26
  178.3 1.3 collective-permute-start.23
  179.6 4.2 %collective-permute-start.22 = (f32[2,76,6]{2,1,0:T(8,128)S(1)}, f32[2,76,6]{2,1,0:T(8,128)S(1)}, u32[]{:S(2)}, u32[]{:S(2)}) collective-permute-start(f32[2,76,6]{2,1,0:T(8,128)S(1)} %get-tuple-element.108), channel_id=1, source_target_pairs={{0,1},{1,2},{2,3},{4,5},{5,6},{6,7},{8,9},{9,10},{10,11},{12,13},{... | collective-permute-start | bytes 10952 | tf_op jit(solution)/shard_map/ppermute | solution.py:32
  185.7 2.1 divide_exponential_fusion
  188.1 2.1 multiply_add_fusion
  192.4 1.3 collective-permute-start.29
  193.7 4.8 %collective-permute-start.28 = (f32[2,3,11]{2,1,0:T(4,128)S(1)}, f32[2,3,11]{2,1,0:T(4,128)S(1)}, u32[]{:S(2)}, u32[]{:S(2)}) collective-permute-start(f32[2,3,11]{2,1,0:T(4,128)S(1)} %get-tuple-element.204), channel_id=1, source_target_pairs={{0,4},{4,8},{8,12},{12,16},{16,20},{20,24},{24,28},{1,5},{5,9},{9,... | collective-permute-start | bytes 800 | tf_op jit(solution)/shard_map/ppermute | solution.py:32
  198.5 1.3 collective-permute-done.28
  201.2 4.5 %collective-permute-start.30 = (f32[2,11,3]{2,1,0:T(8,128)S(1)}, f32[2,11,3]{2,1,0:T(8,128)S(1)}, u32[]{:S(2)}, u32[]{:S(2)}) collective-permute-start(f32[2,11,3]{2,1,0:T(8,128)S(1)} %get-tuple-element.192), channel_id=1, source_target_pairs={{0,1},{1,2},{2,3},{4,5},{5,6},{6,7},{8,9},{9,10},{10,11},{12,13},{... | collective-permute-start | bytes 800 | tf_op jit(solution)/shard_map/ppermute | solution.py:32
  208.7 5.2 %collective-permute-start.32 = (f32[2,2,8]{2,1,0:T(2,128)S(1)}, f32[2,2,8]{2,1,0:T(2,128)S(1)}, u32[]{:S(2)}, u32[]{:S(2)}) collective-permute-start(f32[2,2,8]{2,1,0:T(2,128)S(1)} %get-tuple-element.21), channel_id=1, source_target_pairs={{0,4},{4,8},{8,12},{12,16},{16,20},{20,24},{24,28},{1,5},{5,9},{9,... | collective-permute-start | bytes 392 | tf_op jit(solution)/shard_map/ppermute | solution.py:32
  216.6 5.2 %collective-permute-start.34 = (f32[2,6,2]{2,1,0:T(8,128)S(1)}, f32[2,6,2]{2,1,0:T(8,128)S(1)}, u32[]{:S(2)}, u32[]{:S(2)}) collective-permute-start(f32[2,6,2]{2,1,0:T(8,128)S(1)} %get-tuple-element.202), channel_id=1, source_target_pairs={{0,1},{1,2},{2,3},{4,5},{5,6},{6,7},{8,9},{9,10},{10,11},{12,13},{... | collective-permute-start | bytes 296 | tf_op jit(solution)/shard_map/ppermute | solution.py:32
  223.9 9.7 %all-reduce.17 = (f32[]{:T(128)}, f32[]{:T(128)}) all-reduce(f32[]{:T(128)} %get-tuple-element.20, f32[]{:T(128)} %multiply_reduce_fusion.1), channel_id=1, replica_groups=mesh['ty'=8,'tx'=4] {'tx'}, use_global_device_ids=true, to_apply=%region_14.15 | all-reduce | flops 2 | bytes 16 | tf_op jit(solution)/shard_map/psum | solution.py:179
  233.6 21.3 %all-reduce.13 = (f32[]{:T(128)}, f32[]{:T(128)}) all-reduce(f32[]{:T(128)} %get-tuple-element.12, f32[]{:T(128)} %get-tuple-element.13), channel_id=1, replica_groups=mesh['ty'=8,'tx'=4] {'ty'}, use_global_device_ids=true, to_apply=%region_15.16 | all-reduce | flops 2 | bytes 16 | tf_op jit(solution)/shard_map/psum | solution.py:178
  256.8 1.3 collective-permute-start.37
  258.1 4.5 %collective-permute-start.36 = (f32[2,3,11]{2,1,0:T(4,128)S(1)}, f32[2,3,11]{2,1,0:T(4,128)S(1)}, u32[]{:S(2)}, u32[]{:S(2)}) collective-permute-start(f32[2,3,11]{2,1,0:T(4,128)S(1)} %get-tuple-element.200), channel_id=1, source_target_pairs={{0,4},{4,8},{8,12},{12,16},{16,20},{20,24},{24,28},{1,5},{5,9},{9,... | collective-permute-start | bytes 800 | tf_op jit(solution)/shard_map/ppermute | solution.py:32
  262.7 1.3 collective-permute-done.36
  265.3 3.0 collective-permute-start.38
  271.4 4.8 %collective-permute-start.40 = (f32[2,2,8]{2,1,0:T(2,128)S(1)}, f32[2,2,8]{2,1,0:T(2,128)S(1)}, u32[]{:S(2)}, u32[]{:S(2)}) collective-permute-start(f32[2,2,8]{2,1,0:T(2,128)S(1)} %get-tuple-element.19), channel_id=1, source_target_pairs={{0,4},{4,8},{8,12},{12,16},{16,20},{20,24},{24,28},{1,5},{5,9},{9,... | collective-permute-start | bytes 392 | tf_op jit(solution)/shard_map/ppermute | solution.py:32
  278.9 3.2 %collective-permute-start.42 = (f32[2,6,2]{2,1,0:T(8,128)S(1)}, f32[2,6,2]{2,1,0:T(8,128)S(1)}, u32[]{:S(2)}, u32[]{:S(2)}) collective-permute-start(f32[2,6,2]{2,1,0:T(8,128)S(1)} %get-tuple-element.198), channel_id=1, source_target_pairs={{0,1},{1,2},{2,3},{4,5},{5,6},{6,7},{8,9},{9,10},{10,11},{12,13},{... | collective-permute-start | bytes 296 | tf_op jit(solution)/shard_map/ppermute | solution.py:32
  284.2 9.7 %all-reduce.16 = (f32[]{:T(128)}, f32[]{:T(128)}) all-reduce(f32[]{:T(128)} %get-tuple-element.18, f32[]{:T(128)} %multiply_reduce_fusion), channel_id=1, replica_groups=mesh['ty'=8,'tx'=4] {'tx'}, use_global_device_ids=true, to_apply=%region_20.21 | all-reduce | flops 2 | bytes 16 | tf_op jit(solution)/shard_map/psum | solution.py:179
  294.0 22.0 %all-reduce.12 = (f32[]{:T(128)}, f32[]{:T(128)}) all-reduce(f32[]{:T(128)} %get-tuple-element.10, f32[]{:T(128)} %get-tuple-element.11), channel_id=1, replica_groups=mesh['ty'=8,'tx'=4] {'ty'}, use_global_device_ids=true, to_apply=%region_21.22 | all-reduce | flops 2 | bytes 16 | tf_op jit(solution)/shard_map/psum | solution.py:178
  (165 shorter events, 52.1 us)
Async XLA Ops:
  0.6 9.2 %copy-start.1 = (f32[64,256]{1,0:T(8,128)S(1)}, f32[64,256]{1,0:T(8,128)}, u32[]{:S(2)}) copy-start(f32[64,256]{1,0:T(8,128)} %param.3) | copy-start | bytes 196612
  9.8 21.0 %copy-start.2 = (s32[2,8]{1,0:T(2,128)S(1)}, s32[2,8]{1,0:T(2,128)}, u32[]{:S(2)}) copy-start(s32[2,8]{1,0:T(2,128)} %param.5) | copy-start | bytes 196
  18.3 6.8 %collective-permute-start.1 = (f32[2,6,128]{2,1,0:T(8,128)S(1)}, f32[2,6,128]{2,1,0:T(8,128)S(1)}, u32[]{:S(2)}, u32[]{:S(2)}) collective-permute-start(f32[2,6,128]{2,1,0:T(8,128)S(1)} %get-tuple-element.189), channel_id=1, source_target_pairs={{4,0},{8,4},{12,8},{16,12},{20,16},{24,20},{28,24},{5,1},{9,5},{13... | collective-permute-start | bytes 18440 | tf_op jit(solution)/shard_map/ppermute | solution.py:35
  19.6 6.8 %collective-permute-start = (f32[2,6,128]{2,1,0:T(8,128)S(1)}, f32[2,6,128]{2,1,0:T(8,128)S(1)}, u32[]{:S(2)}, u32[]{:S(2)}) collective-permute-start(f32[2,6,128]{2,1,0:T(8,128)S(1)} %get-tuple-element.188), channel_id=1, source_target_pairs={{0,4},{4,8},{8,12},{12,16},{16,20},{20,24},{24,28},{1,5},{5,9},{9,... | collective-permute-start | bytes 18440 | tf_op jit(solution)/shard_map/ppermute | solution.py:32
  26.5 4.6 %collective-permute-start.3 = (f32[2,44,6]{2,1,0:T(8,128)S(1)}, f32[2,44,6]{2,1,0:T(8,128)S(1)}, u32[]{:S(2)}, u32[]{:S(2)}) collective-permute-start(f32[2,44,6]{2,1,0:T(8,128)S(1)} %get-tuple-element.176), channel_id=1, source_target_pairs={{1,0},{2,1},{3,2},{5,4},{6,5},{7,6},{9,8},{10,9},{11,10},{13,12},{... | collective-permute-start | bytes 6344 | tf_op jit(solution)/shard_map/ppermute | solution.py:35
  27.8 3.9 %collective-permute-start.2 = (f32[2,44,6]{2,1,0:T(8,128)S(1)}, f32[2,44,6]{2,1,0:T(8,128)S(1)}, u32[]{:S(2)}, u32[]{:S(2)}) collective-permute-start(f32[2,44,6]{2,1,0:T(8,128)S(1)} %get-tuple-element.175), channel_id=1, source_target_pairs={{0,1},{1,2},{2,3},{4,5},{5,6},{6,7},{8,9},{9,10},{10,11},{12,13},{... | collective-permute-start | bytes 6344 | tf_op jit(solution)/shard_map/ppermute | solution.py:32
  33.2 23.4 %copy-start = (f32[64,256]{1,0:T(8,128)S(1)}, f32[64,256]{1,0:T(8,128)}, u32[]{:S(2)}) copy-start(f32[64,256]{1,0:T(8,128)} %param.4) | copy-start | bytes 196612
  35.2 6.8 %collective-permute-start.5 = (f32[2,3,11]{2,1,0:T(4,128)S(1)}, f32[2,3,11]{2,1,0:T(4,128)S(1)}, u32[]{:S(2)}, u32[]{:S(2)}) collective-permute-start(f32[2,3,11]{2,1,0:T(4,128)S(1)} %get-tuple-element.215), channel_id=1, source_target_pairs={{4,0},{8,4},{12,8},{16,12},{20,16},{24,20},{28,24},{5,1},{9,5},{13... | collective-permute-start | bytes 800 | tf_op jit(solution)/shard_map/ppermute | solution.py:35
  36.5 6.8 %collective-permute-start.4 = (f32[2,3,11]{2,1,0:T(4,128)S(1)}, f32[2,3,11]{2,1,0:T(4,128)S(1)}, u32[]{:S(2)}, u32[]{:S(2)}) collective-permute-start(f32[2,3,11]{2,1,0:T(4,128)S(1)} %get-tuple-element.214), channel_id=1, source_target_pairs={{0,4},{4,8},{8,12},{12,16},{16,20},{20,24},{24,28},{1,5},{5,9},{9,... | collective-permute-start | bytes 800 | tf_op jit(solution)/shard_map/ppermute | solution.py:32
  43.4 4.4 %collective-permute-start.7 = (f32[2,11,3]{2,1,0:T(8,128)S(1)}, f32[2,11,3]{2,1,0:T(8,128)S(1)}, u32[]{:S(2)}, u32[]{:S(2)}) collective-permute-start(f32[2,11,3]{2,1,0:T(8,128)S(1)} %get-tuple-element.197), channel_id=1, source_target_pairs={{1,0},{2,1},{3,2},{5,4},{6,5},{7,6},{9,8},{10,9},{11,10},{13,12},{... | collective-permute-start | bytes 800 | tf_op jit(solution)/shard_map/ppermute | solution.py:35
  44.7 3.9 %collective-permute-start.6 = (f32[2,11,3]{2,1,0:T(8,128)S(1)}, f32[2,11,3]{2,1,0:T(8,128)S(1)}, u32[]{:S(2)}, u32[]{:S(2)}) collective-permute-start(f32[2,11,3]{2,1,0:T(8,128)S(1)} %get-tuple-element.196), channel_id=1, source_target_pairs={{0,1},{1,2},{2,3},{4,5},{5,6},{6,7},{8,9},{9,10},{10,11},{12,13},{... | collective-permute-start | bytes 800 | tf_op jit(solution)/shard_map/ppermute | solution.py:32
  49.5 7.0 %collective-permute-start.9 = (f32[2,2,8]{2,1,0:T(2,128)S(1)}, f32[2,2,8]{2,1,0:T(2,128)S(1)}, u32[]{:S(2)}, u32[]{:S(2)}) collective-permute-start(f32[2,2,8]{2,1,0:T(2,128)S(1)} %get-tuple-element.44), channel_id=1, source_target_pairs={{4,0},{8,4},{12,8},{16,12},{20,16},{24,20},{28,24},{5,1},{9,5},{13... | collective-permute-start | bytes 392 | tf_op jit(solution)/shard_map/ppermute | solution.py:35
  50.8 7.0 %collective-permute-start.8 = (f32[2,2,8]{2,1,0:T(2,128)S(1)}, f32[2,2,8]{2,1,0:T(2,128)S(1)}, u32[]{:S(2)}, u32[]{:S(2)}) collective-permute-start(f32[2,2,8]{2,1,0:T(2,128)S(1)} %get-tuple-element.44), channel_id=1, source_target_pairs={{0,4},{4,8},{8,12},{12,16},{16,20},{20,24},{24,28},{1,5},{5,9},{9,... | collective-permute-start | bytes 392 | tf_op jit(solution)/shard_map/ppermute | solution.py:32
  57.9 6.2 %collective-permute-start.11 = (f32[2,6,2]{2,1,0:T(8,128)S(1)}, f32[2,6,2]{2,1,0:T(8,128)S(1)}, u32[]{:S(2)}, u32[]{:S(2)}) collective-permute-start(f32[2,6,2]{2,1,0:T(8,128)S(1)} %get-tuple-element.213), channel_id=1, source_target_pairs={{1,0},{2,1},{3,2},{5,4},{6,5},{7,6},{9,8},{10,9},{11,10},{13,12},{... | collective-permute-start | bytes 296 | tf_op jit(solution)/shard_map/ppermute | solution.py:35
  59.2 5.7 %collective-permute-start.10 = (f32[2,6,2]{2,1,0:T(8,128)S(1)}, f32[2,6,2]{2,1,0:T(8,128)S(1)}, u32[]{:S(2)}, u32[]{:S(2)}) collective-permute-start(f32[2,6,2]{2,1,0:T(8,128)S(1)} %get-tuple-element.212), channel_id=1, source_target_pairs={{0,1},{1,2},{2,3},{4,5},{5,6},{6,7},{8,9},{9,10},{10,11},{12,13},{... | collective-permute-start | bytes 296 | tf_op jit(solution)/shard_map/ppermute | solution.py:32
  102.8 11.7 %collective-permute-start.13 = (f32[2,3,11]{2,1,0:T(4,128)S(1)}, f32[2,3,11]{2,1,0:T(4,128)S(1)}, u32[]{:S(2)}, u32[]{:S(2)}) collective-permute-start(f32[2,3,11]{2,1,0:T(4,128)S(1)} %get-tuple-element.211), channel_id=1, source_target_pairs={{4,0},{8,4},{12,8},{16,12},{20,16},{24,20},{28,24},{5,1},{9,5},{13... | collective-permute-start | bytes 800 | tf_op jit(solution)/shard_map/ppermute | solution.py:35
  104.1 10.4 %collective-permute-start.12 = (f32[2,3,11]{2,1,0:T(4,128)S(1)}, f32[2,3,11]{2,1,0:T(4,128)S(1)}, u32[]{:S(2)}, u32[]{:S(2)}) collective-permute-start(f32[2,3,11]{2,1,0:T(4,128)S(1)} %get-tuple-element.210), channel_id=1, source_target_pairs={{0,4},{4,8},{8,12},{12,16},{16,20},{20,24},{24,28},{1,5},{5,9},{9,... | collective-permute-start | bytes 800 | tf_op jit(solution)/shard_map/ppermute | solution.py:32
  108.7 69.5 %collective-permute-start.21 = (f32[2,6,256]{2,1,0:T(8,128)S(1)}, f32[2,6,256]{2,1,0:T(8,128)S(1)}, u32[]{:S(2)}, u32[]{:S(2)}) collective-permute-start(f32[2,6,256]{2,1,0:T(8,128)S(1)} %get-tuple-element.111), channel_id=1, source_target_pairs={{4,0},{8,4},{12,8},{16,12},{20,16},{24,20},{28,24},{5,1},{9,5},{13... | collective-permute-start | bytes 36872 | tf_op jit(solution)/shard_map/ppermute | solution.py:35
  110.0 68.2 %collective-permute-start.20 = (f32[2,6,256]{2,1,0:T(8,128)S(1)}, f32[2,6,256]{2,1,0:T(8,128)S(1)}, u32[]{:S(2)}, u32[]{:S(2)}) collective-permute-start(f32[2,6,256]{2,1,0:T(8,128)S(1)} %get-tuple-element.110), channel_id=1, source_target_pairs={{0,4},{4,8},{8,12},{12,16},{16,20},{20,24},{24,28},{1,5},{5,9},{9,... | collective-permute-start | bytes 36872 | tf_op jit(solution)/shard_map/ppermute | solution.py:32
  114.7 4.3 %collective-permute-start.15 = (f32[2,11,3]{2,1,0:T(8,128)S(1)}, f32[2,11,3]{2,1,0:T(8,128)S(1)}, u32[]{:S(2)}, u32[]{:S(2)}) collective-permute-start(f32[2,11,3]{2,1,0:T(8,128)S(1)} %get-tuple-element.195), channel_id=1, source_target_pairs={{1,0},{2,1},{3,2},{5,4},{6,5},{7,6},{9,8},{10,9},{11,10},{13,12},{... | collective-permute-start | bytes 800 | tf_op jit(solution)/shard_map/ppermute | solution.py:35
  115.9 3.9 %collective-permute-start.14 = (f32[2,11,3]{2,1,0:T(8,128)S(1)}, f32[2,11,3]{2,1,0:T(8,128)S(1)}, u32[]{:S(2)}, u32[]{:S(2)}) collective-permute-start(f32[2,11,3]{2,1,0:T(8,128)S(1)} %get-tuple-element.194), channel_id=1, source_target_pairs={{0,1},{1,2},{2,3},{4,5},{5,6},{6,7},{8,9},{9,10},{10,11},{12,13},{... | collective-permute-start | bytes 800 | tf_op jit(solution)/shard_map/ppermute | solution.py:32
  120.7 5.9 %collective-permute-start.17 = (f32[2,2,8]{2,1,0:T(2,128)S(1)}, f32[2,2,8]{2,1,0:T(2,128)S(1)}, u32[]{:S(2)}, u32[]{:S(2)}) collective-permute-start(f32[2,2,8]{2,1,0:T(2,128)S(1)} %get-tuple-element.42), channel_id=1, source_target_pairs={{4,0},{8,4},{12,8},{16,12},{20,16},{24,20},{28,24},{5,1},{9,5},{13... | collective-permute-start | bytes 392 | tf_op jit(solution)/shard_map/ppermute | solution.py:35
  122.0 5.8 %collective-permute-start.16 = (f32[2,2,8]{2,1,0:T(2,128)S(1)}, f32[2,2,8]{2,1,0:T(2,128)S(1)}, u32[]{:S(2)}, u32[]{:S(2)}) collective-permute-start(f32[2,2,8]{2,1,0:T(2,128)S(1)} %get-tuple-element.42), channel_id=1, source_target_pairs={{0,4},{4,8},{8,12},{12,16},{16,20},{20,24},{24,28},{1,5},{5,9},{9,... | collective-permute-start | bytes 392 | tf_op jit(solution)/shard_map/ppermute | solution.py:32
  128.0 4.3 %collective-permute-start.19 = (f32[2,6,2]{2,1,0:T(8,128)S(1)}, f32[2,6,2]{2,1,0:T(8,128)S(1)}, u32[]{:S(2)}, u32[]{:S(2)}) collective-permute-start(f32[2,6,2]{2,1,0:T(8,128)S(1)} %get-tuple-element.209), channel_id=1, source_target_pairs={{1,0},{2,1},{3,2},{5,4},{6,5},{7,6},{9,8},{10,9},{11,10},{13,12},{... | collective-permute-start | bytes 296 | tf_op jit(solution)/shard_map/ppermute | solution.py:35
  129.2 3.8 %collective-permute-start.18 = (f32[2,6,2]{2,1,0:T(8,128)S(1)}, f32[2,6,2]{2,1,0:T(8,128)S(1)}, u32[]{:S(2)}, u32[]{:S(2)}) collective-permute-start(f32[2,6,2]{2,1,0:T(8,128)S(1)} %get-tuple-element.208), channel_id=1, source_target_pairs={{0,1},{1,2},{2,3},{4,5},{5,6},{6,7},{8,9},{9,10},{10,11},{12,13},{... | collective-permute-start | bytes 296 | tf_op jit(solution)/shard_map/ppermute | solution.py:32
  165.6 6.1 %collective-permute-start.25 = (f32[2,2,8]{2,1,0:T(2,128)S(1)}, f32[2,2,8]{2,1,0:T(2,128)S(1)}, u32[]{:S(2)}, u32[]{:S(2)}) collective-permute-start(f32[2,2,8]{2,1,0:T(2,128)S(1)} %multiply_subtract_fusion.4), channel_id=1, source_target_pairs={{4,0},{8,4},{12,8},{16,12},{20,16},{24,20},{28,24},{5,1},{9,5},{13... | collective-permute-start | bytes 392 | tf_op jit(solution)/shard_map/ppermute | solution.py:35
  166.9 5.8 %collective-permute-start.24 = (f32[2,2,8]{2,1,0:T(2,128)S(1)}, f32[2,2,8]{2,1,0:T(2,128)S(1)}, u32[]{:S(2)}, u32[]{:S(2)}) collective-permute-start(f32[2,2,8]{2,1,0:T(2,128)S(1)} %multiply_subtract_fusion.4), channel_id=1, source_target_pairs={{0,4},{4,8},{8,12},{12,16},{16,20},{20,24},{24,28},{1,5},{5,9},{9,... | collective-permute-start | bytes 392 | tf_op jit(solution)/shard_map/ppermute | solution.py:32
  172.8 4.3 %collective-permute-start.27 = (f32[2,6,2]{2,1,0:T(8,128)S(1)}, f32[2,6,2]{2,1,0:T(8,128)S(1)}, u32[]{:S(2)}, u32[]{:S(2)}) collective-permute-start(f32[2,6,2]{2,1,0:T(8,128)S(1)} %get-tuple-element.207), channel_id=1, source_target_pairs={{1,0},{2,1},{3,2},{5,4},{6,5},{7,6},{9,8},{10,9},{11,10},{13,12},{... | collective-permute-start | bytes 296 | tf_op jit(solution)/shard_map/ppermute | solution.py:35
  174.1 3.8 %collective-permute-start.26 = (f32[2,6,2]{2,1,0:T(8,128)S(1)}, f32[2,6,2]{2,1,0:T(8,128)S(1)}, u32[]{:S(2)}, u32[]{:S(2)}) collective-permute-start(f32[2,6,2]{2,1,0:T(8,128)S(1)} %get-tuple-element.206), channel_id=1, source_target_pairs={{0,1},{1,2},{2,3},{4,5},{5,6},{6,7},{8,9},{9,10},{10,11},{12,13},{... | collective-permute-start | bytes 296 | tf_op jit(solution)/shard_map/ppermute | solution.py:32
  178.3 5.9 %collective-permute-start.23 = (f32[2,76,6]{2,1,0:T(8,128)S(1)}, f32[2,76,6]{2,1,0:T(8,128)S(1)}, u32[]{:S(2)}, u32[]{:S(2)}) collective-permute-start(f32[2,76,6]{2,1,0:T(8,128)S(1)} %get-tuple-element.109), channel_id=1, source_target_pairs={{1,0},{2,1},{3,2},{5,4},{6,5},{7,6},{9,8},{10,9},{11,10},{13,12},{... | collective-permute-start | bytes 10952 | tf_op jit(solution)/shard_map/ppermute | solution.py:35
  179.6 4.9 %collective-permute-start.22 = (f32[2,76,6]{2,1,0:T(8,128)S(1)}, f32[2,76,6]{2,1,0:T(8,128)S(1)}, u32[]{:S(2)}, u32[]{:S(2)}) collective-permute-start(f32[2,76,6]{2,1,0:T(8,128)S(1)} %get-tuple-element.108), channel_id=1, source_target_pairs={{0,1},{1,2},{2,3},{4,5},{5,6},{6,7},{8,9},{9,10},{10,11},{12,13},{... | collective-permute-start | bytes 10952 | tf_op jit(solution)/shard_map/ppermute | solution.py:32
  192.4 6.1 %collective-permute-start.29 = (f32[2,3,11]{2,1,0:T(4,128)S(1)}, f32[2,3,11]{2,1,0:T(4,128)S(1)}, u32[]{:S(2)}, u32[]{:S(2)}) collective-permute-start(f32[2,3,11]{2,1,0:T(4,128)S(1)} %get-tuple-element.205), channel_id=1, source_target_pairs={{4,0},{8,4},{12,8},{16,12},{20,16},{24,20},{28,24},{5,1},{9,5},{13... | collective-permute-start | bytes 800 | tf_op jit(solution)/shard_map/ppermute | solution.py:35
  193.7 6.1 %collective-permute-start.28 = (f32[2,3,11]{2,1,0:T(4,128)S(1)}, f32[2,3,11]{2,1,0:T(4,128)S(1)}, u32[]{:S(2)}, u32[]{:S(2)}) collective-permute-start(f32[2,3,11]{2,1,0:T(4,128)S(1)} %get-tuple-element.204), channel_id=1, source_target_pairs={{0,4},{4,8},{8,12},{12,16},{16,20},{20,24},{24,28},{1,5},{5,9},{9,... | collective-permute-start | bytes 800 | tf_op jit(solution)/shard_map/ppermute | solution.py:32
  199.9 5.8 %collective-permute-start.31 = (f32[2,11,3]{2,1,0:T(8,128)S(1)}, f32[2,11,3]{2,1,0:T(8,128)S(1)}, u32[]{:S(2)}, u32[]{:S(2)}) collective-permute-start(f32[2,11,3]{2,1,0:T(8,128)S(1)} %get-tuple-element.193), channel_id=1, source_target_pairs={{1,0},{2,1},{3,2},{5,4},{6,5},{7,6},{9,8},{10,9},{11,10},{13,12},{... | collective-permute-start | bytes 800 | tf_op jit(solution)/shard_map/ppermute | solution.py:35
  201.2 5.4 %collective-permute-start.30 = (f32[2,11,3]{2,1,0:T(8,128)S(1)}, f32[2,11,3]{2,1,0:T(8,128)S(1)}, u32[]{:S(2)}, u32[]{:S(2)}) collective-permute-start(f32[2,11,3]{2,1,0:T(8,128)S(1)} %get-tuple-element.192), channel_id=1, source_target_pairs={{0,1},{1,2},{2,3},{4,5},{5,6},{6,7},{8,9},{9,10},{10,11},{12,13},{... | collective-permute-start | bytes 800 | tf_op jit(solution)/shard_map/ppermute | solution.py:32
  207.4 6.5 %collective-permute-start.33 = (f32[2,2,8]{2,1,0:T(2,128)S(1)}, f32[2,2,8]{2,1,0:T(2,128)S(1)}, u32[]{:S(2)}, u32[]{:S(2)}) collective-permute-start(f32[2,2,8]{2,1,0:T(2,128)S(1)} %get-tuple-element.21), channel_id=1, source_target_pairs={{4,0},{8,4},{12,8},{16,12},{20,16},{24,20},{28,24},{5,1},{9,5},{13... | collective-permute-start | bytes 392 | tf_op jit(solution)/shard_map/ppermute | solution.py:35
  208.7 6.5 %collective-permute-start.32 = (f32[2,2,8]{2,1,0:T(2,128)S(1)}, f32[2,2,8]{2,1,0:T(2,128)S(1)}, u32[]{:S(2)}, u32[]{:S(2)}) collective-permute-start(f32[2,2,8]{2,1,0:T(2,128)S(1)} %get-tuple-element.21), channel_id=1, source_target_pairs={{0,4},{4,8},{8,12},{12,16},{16,20},{20,24},{24,28},{1,5},{5,9},{9,... | collective-permute-start | bytes 392 | tf_op jit(solution)/shard_map/ppermute | solution.py:32
  215.3 6.5 %collective-permute-start.35 = (f32[2,6,2]{2,1,0:T(8,128)S(1)}, f32[2,6,2]{2,1,0:T(8,128)S(1)}, u32[]{:S(2)}, u32[]{:S(2)}) collective-permute-start(f32[2,6,2]{2,1,0:T(8,128)S(1)} %get-tuple-element.203), channel_id=1, source_target_pairs={{1,0},{2,1},{3,2},{5,4},{6,5},{7,6},{9,8},{10,9},{11,10},{13,12},{... | collective-permute-start | bytes 296 | tf_op jit(solution)/shard_map/ppermute | solution.py:35
  216.6 6.0 %collective-permute-start.34 = (f32[2,6,2]{2,1,0:T(8,128)S(1)}, f32[2,6,2]{2,1,0:T(8,128)S(1)}, u32[]{:S(2)}, u32[]{:S(2)}) collective-permute-start(f32[2,6,2]{2,1,0:T(8,128)S(1)} %get-tuple-element.202), channel_id=1, source_target_pairs={{0,1},{1,2},{2,3},{4,5},{5,6},{6,7},{8,9},{9,10},{10,11},{12,13},{... | collective-permute-start | bytes 296 | tf_op jit(solution)/shard_map/ppermute | solution.py:32
  256.8 5.9 %collective-permute-start.37 = (f32[2,3,11]{2,1,0:T(4,128)S(1)}, f32[2,3,11]{2,1,0:T(4,128)S(1)}, u32[]{:S(2)}, u32[]{:S(2)}) collective-permute-start(f32[2,3,11]{2,1,0:T(4,128)S(1)} %get-tuple-element.201), channel_id=1, source_target_pairs={{4,0},{8,4},{12,8},{16,12},{20,16},{24,20},{28,24},{5,1},{9,5},{13... | collective-permute-start | bytes 800 | tf_op jit(solution)/shard_map/ppermute | solution.py:35
  258.1 5.9 %collective-permute-start.36 = (f32[2,3,11]{2,1,0:T(4,128)S(1)}, f32[2,3,11]{2,1,0:T(4,128)S(1)}, u32[]{:S(2)}, u32[]{:S(2)}) collective-permute-start(f32[2,3,11]{2,1,0:T(4,128)S(1)} %get-tuple-element.200), channel_id=1, source_target_pairs={{0,4},{4,8},{8,12},{12,16},{16,20},{20,24},{24,28},{1,5},{5,9},{9,... | collective-permute-start | bytes 800 | tf_op jit(solution)/shard_map/ppermute | solution.py:32
  264.0 4.3 %collective-permute-start.39 = (f32[2,11,3]{2,1,0:T(8,128)S(1)}, f32[2,11,3]{2,1,0:T(8,128)S(1)}, u32[]{:S(2)}, u32[]{:S(2)}) collective-permute-start(f32[2,11,3]{2,1,0:T(8,128)S(1)} %get-tuple-element.191), channel_id=1, source_target_pairs={{1,0},{2,1},{3,2},{5,4},{6,5},{7,6},{9,8},{10,9},{11,10},{13,12},{... | collective-permute-start | bytes 800 | tf_op jit(solution)/shard_map/ppermute | solution.py:35
  265.3 3.9 %collective-permute-start.38 = (f32[2,11,3]{2,1,0:T(8,128)S(1)}, f32[2,11,3]{2,1,0:T(8,128)S(1)}, u32[]{:S(2)}, u32[]{:S(2)}) collective-permute-start(f32[2,11,3]{2,1,0:T(8,128)S(1)} %get-tuple-element.190), channel_id=1, source_target_pairs={{0,1},{1,2},{2,3},{4,5},{5,6},{6,7},{8,9},{9,10},{10,11},{12,13},{... | collective-permute-start | bytes 800 | tf_op jit(solution)/shard_map/ppermute | solution.py:32
  270.1 6.1 %collective-permute-start.41 = (f32[2,2,8]{2,1,0:T(2,128)S(1)}, f32[2,2,8]{2,1,0:T(2,128)S(1)}, u32[]{:S(2)}, u32[]{:S(2)}) collective-permute-start(f32[2,2,8]{2,1,0:T(2,128)S(1)} %get-tuple-element.19), channel_id=1, source_target_pairs={{4,0},{8,4},{12,8},{16,12},{20,16},{24,20},{28,24},{5,1},{9,5},{13... | collective-permute-start | bytes 392 | tf_op jit(solution)/shard_map/ppermute | solution.py:35
  271.4 6.1 %collective-permute-start.40 = (f32[2,2,8]{2,1,0:T(2,128)S(1)}, f32[2,2,8]{2,1,0:T(2,128)S(1)}, u32[]{:S(2)}, u32[]{:S(2)}) collective-permute-start(f32[2,2,8]{2,1,0:T(2,128)S(1)} %get-tuple-element.19), channel_id=1, source_target_pairs={{0,4},{4,8},{8,12},{12,16},{16,20},{20,24},{24,28},{1,5},{5,9},{9,... | collective-permute-start | bytes 392 | tf_op jit(solution)/shard_map/ppermute | solution.py:32
  277.6 4.5 %collective-permute-start.43 = (f32[2,6,2]{2,1,0:T(8,128)S(1)}, f32[2,6,2]{2,1,0:T(8,128)S(1)}, u32[]{:S(2)}, u32[]{:S(2)}) collective-permute-start(f32[2,6,2]{2,1,0:T(8,128)S(1)} %get-tuple-element.199), channel_id=1, source_target_pairs={{1,0},{2,1},{3,2},{5,4},{6,5},{7,6},{9,8},{10,9},{11,10},{13,12},{... | collective-permute-start | bytes 296 | tf_op jit(solution)/shard_map/ppermute | solution.py:35
  278.9 4.1 %collective-permute-start.42 = (f32[2,6,2]{2,1,0:T(8,128)S(1)}, f32[2,6,2]{2,1,0:T(8,128)S(1)}, u32[]{:S(2)}, u32[]{:S(2)}) collective-permute-start(f32[2,6,2]{2,1,0:T(8,128)S(1)} %get-tuple-element.198), channel_id=1, source_target_pairs={{0,1},{1,2},{2,3},{4,5},{5,6},{6,7},{8,9},{9,10},{10,11},{12,13},{... | collective-permute-start | bytes 296 | tf_op jit(solution)/shard_map/ppermute | solution.py:32
